TPU v7x, 128 devices: a whole 4x4x4 slice. The times are simulated.
128 devices in a mesh: depth: 4 (over z_lo, core), inw: 8 (over z_hi, x), outw: 4 (over y).
Axes of the slice: x: 4, y: 4, z: 4 (z_hi: 2, z_lo: 2; z = z_hi * 2 + z_lo), core: 2. Of those that a mesh axis runs over, the one named last changes fastest.
Arguments:
- inputs: bfloat16 [1536, 8192], P(('depth', 'inw'), 'outw'), may hold values from -6 to 6
- w_gate: bfloat16 [8192, 14336], P(('outw', 'depth'), 'inw'), may hold values from -0.0625 to 0.0625
- w_up: bfloat16 [8192, 14336], P(('outw', 'depth'), 'inw'), may hold values from -0.0625 to 0.0625
- w_down: bfloat16 [14336, 8192], P('inw', ('outw', 'depth')), may hold values from -0.046875 to 0.046875
- cotangent: bfloat16 [1536, 8192], P(('depth', 'inw'), 'outw'), may hold values from -1.5 to 1.5
Outputs:
- outputs: bfloat16 [1536, 8192], P(('depth', 'inw'), 'outw')
- grad_inputs: bfloat16 [1536, 8192], P(('depth', 'inw'), 'outw')
- grad_gate: bfloat16 [8192, 14336], P(('outw', 'depth'), 'inw')
- grad_up: bfloat16 [8192, 14336], P(('outw', 'depth'), 'inw')
- grad_down: bfloat16 [14336, 8192], P('inw', ('outw', 'depth'))
All inputs are finite; a program needn't handle non-finite values.
Results may differ from a plain program's by a relative error of at most 0.027.
Values may be sent and summed in bfloat16 or wider, within the bound.
No kernel may reach another device: no remote copies, remote signals or barrier semaphores. Data moves between devices by JAX's collectives and lax.ppermute only.
A program may use at most 128 MiB of HBM per device.

v0:
```python
import jax
import jax.numpy as jnp
from jax import lax
from jax.sharding import PartitionSpec as P


def matmul(left, right):
    return jnp.dot(left, right, preferred_element_type=jnp.float32)


def times_transposed(left, right):
    return lax.dot_general(
        left, right, (((1,), (1,)), ((), ())), preferred_element_type=jnp.float32
    )


def over_tokens(left, right):
    return lax.dot_general(
        left, right, (((0,), (0,)), ((), ())), preferred_element_type=jnp.float32
    )


def gate_grads(grad_hidden, gate_sum, up_sum):
    sigmoid_gate = jax.nn.sigmoid(gate_sum)
    grad_gate_act = (
        grad_hidden * up_sum * sigmoid_gate * (1.0 + gate_sum * (1.0 - sigmoid_gate))
    ).astype(jnp.bfloat16)
    grad_up_act = (grad_hidden * gate_sum * sigmoid_gate).astype(jnp.bfloat16)
    return (grad_gate_act, grad_up_act)


def body(inputs, w_gate, w_up, w_down, cotangent):
    input_rows = lax.all_gather(inputs, "inw", axis=0, tiled=True)
    gate_full, up_full = (
        lax.all_gather(w_gate, "depth", axis=0, tiled=True),
        lax.all_gather(w_up, "depth", axis=0, tiled=True),
    )
    down_full = lax.all_gather(w_down, "depth", axis=1, tiled=True)
    gate_part = matmul(input_rows, gate_full)
    up_part = matmul(input_rows, up_full)
    gate_sum, up_sum = (
        lax.psum_scatter(
            gate_part.astype(jnp.bfloat16), "outw", scatter_dimension=0, tiled=True
        ).astype(jnp.float32),
        lax.psum_scatter(
            up_part.astype(jnp.bfloat16), "outw", scatter_dimension=0, tiled=True
        ).astype(jnp.float32),
    )
    hidden_local = (jax.nn.silu(gate_sum) * up_sum).astype(jnp.bfloat16)
    hidden_all = lax.all_gather(hidden_local, "outw", axis=0, tiled=True)
    output_part = matmul(hidden_all, down_full)
    outputs = lax.psum_scatter(
        output_part.astype(jnp.bfloat16), "inw", scatter_dimension=0, tiled=True
    )
    cot_rows = lax.all_gather(cotangent, "inw", axis=0, tiled=True)
    hidden_part = times_transposed(cot_rows, down_full)
    grad_hidden = lax.psum_scatter(
        hidden_part.astype(jnp.bfloat16), "outw", scatter_dimension=0, tiled=True
    ).astype(jnp.float32)
    gate_act_local, up_act_local = gate_grads(grad_hidden, gate_sum, up_sum)
    gate_act_all, up_act_all = (
        lax.all_gather(gate_act_local, "outw", axis=0, tiled=True),
        lax.all_gather(up_act_local, "outw", axis=0, tiled=True),
    )
    input_part = times_transposed(gate_act_all, gate_full) + times_transposed(up_act_all, up_full)
    grad_inputs = lax.psum_scatter(
        input_part.astype(jnp.bfloat16), "inw", scatter_dimension=0, tiled=True
    )
    gate_weight_part = over_tokens(input_rows, gate_act_all)
    up_weight_part = over_tokens(input_rows, up_act_all)
    grad_gate, grad_up = (
        lax.psum_scatter(
            gate_weight_part.astype(jnp.bfloat16), "depth", scatter_dimension=0, tiled=True
        ).astype(jnp.float32),
        lax.psum_scatter(
            up_weight_part.astype(jnp.bfloat16), "depth", scatter_dimension=0, tiled=True
        ).astype(jnp.float32),
    )
    down_weight_part = over_tokens(hidden_all, cot_rows)
    grad_down = lax.psum_scatter(
        down_weight_part.astype(jnp.bfloat16), "depth", scatter_dimension=1, tiled=True
    )
    return (
        outputs,
        grad_inputs,
        grad_gate.astype(jnp.bfloat16),
        grad_up.astype(jnp.bfloat16),
        grad_down,
    )


def solution(mesh):
    in_specs = (
        P(("depth", "inw"), "outw"),
        P(("outw", "depth"), "inw"),
        P(("outw", "depth"), "inw"),
        P("inw", ("outw", "depth")),
        P(("depth", "inw"), "outw"),
    )
    out_specs = (
        P(("depth", "inw"), "outw"),
        P(("depth", "inw"), "outw"),
        P(("outw", "depth"), "inw"),
        P(("outw", "depth"), "inw"),
        P("inw", ("outw", "depth")),
    )
    return jax.shard_map(body, mesh=mesh, in_specs=in_specs, out_specs=out_specs, check_vma=False)
```

profile of v0, /device:TPU:0, one launch (start us, length us, event | category | flops | bytes accessed | tf_op | source)
XLA Modules:
  0.0 893.0 jit_solution(7045759482686963319)
XLA Ops:
  7.2 0.0 all-gather.9.cloned.1.call-start
  7.2 0.7 all-gather.9.cloned.1.call-update
  7.9 0.0 all-gather.11.cloned.1.call-start
  7.9 0.7 all-gather.11.cloned.1.call-update
  8.6 0.0 all-gather.19.cloned.1.call-start
  8.7 0.7 all-gather.19.cloned.1.call-update
  9.4 0.0 all-gather.17.cloned.1.call-start
  9.4 0.5 all-gather.17.cloned.1.call-update
  10.0 0.0 all-gather.13.cloned.1.call-start
  10.0 0.5 all-gather.13.cloned.1.call-update
  10.5 0.0 reduce-scatter.9.cloned.1.call-start
  10.6 53.5 %all-gather.9.cloned.1.call-done = bf16[384,2048]{1,0:T(8,128)(2,1)} async-done(((bf16[48,2048]{1,0:T(8,128)(2,1)}), bf16[384,2048]{1,0:T(8,128)(2,1)}) %all-gather.9.cloned.1.call-update) | async-done | bytes 1572880 | tf_op jit(solution)/shard_map/all_gather | solution.py:33
  64.1 72.0 %all-gather.11.cloned.1.call-done = bf16[2048,1792]{1,0:T(8,128)(2,1)} async-done(((bf16[512,1792]{1,0:T(8,128)(2,1)}), bf16[2048,1792]{1,0:T(8,128)(2,1)}) %all-gather.11.cloned.1.call-update) | async-done | bytes 7340048 | tf_op jit(solution)/shard_map/all_gather | solution.py:35
  136.1 7.6 convolution_convert_fusion.6
  143.7 0.0 reduce-scatter.9.cloned.1.call-update
  143.7 0.0 reduce-scatter.15.cloned.1.call-start
  143.8 47.8 %all-gather.19.cloned.1.call-done = bf16[384,2048]{1,0:T(8,128)(2,1)} async-done(((bf16[48,2048]{1,0:T(8,128)(2,1)}), bf16[384,2048]{1,0:T(8,128)(2,1)}) %all-gather.19.cloned.1.call-update) | async-done | bytes 1572880 | tf_op jit(solution)/shard_map/all_gather | solution.py:55
  191.6 71.8 %all-gather.17.cloned.1.call-done = bf16[1792,2048]{1,0:T(8,128)(2,1)} async-done(((bf16[1792,512]{1,0:T(8,128)(2,1)}), bf16[1792,2048]{1,0:T(8,128)(2,1)}) %all-gather.17.cloned.1.call-update) | async-done | bytes 7340048 | tf_op jit(solution)/shard_map/all_gather | solution.py:38
  263.4 7.7 convolution_convert_fusion.3
  271.1 0.0 reduce-scatter.15.cloned.1.call-update
  271.2 0.0 reduce-scatter.11.cloned.1.call-start
  271.2 67.4 %all-gather.13.cloned.1.call-done = bf16[2048,1792]{1,0:T(8,128)(2,1)} async-done(((bf16[512,1792]{1,0:T(8,128)(2,1)}), bf16[2048,1792]{1,0:T(8,128)(2,1)}) %all-gather.13.cloned.1.call-update) | async-done | bytes 7340048 | tf_op jit(solution)/shard_map/all_gather | solution.py:36
  338.6 0.0 copy-done.1
  338.6 7.1 convolution_convert_fusion.5
  345.8 0.0 reduce-scatter.11.cloned.1.call-update
  345.8 0.0 all-gather.21.cloned.1.call-start
  345.8 22.4 %reduce-scatter.9.cloned.1.call-done = bf16[96,1792]{1,0:T(8,128)(2,1)} async-done(((bf16[384,1792]{1,0:T(8,128)(2,1)}), bf16[96,1792]{1,0:T(8,128)(2,1)}) %reduce-scatter.9.cloned.1.call-update) | async-done | bytes 344080 | tf_op jit(solution)/shard_map/reduce_scatter | solution.py:42
  368.2 27.7 %reduce-scatter.15.cloned.1.call-done = bf16[96,1792]{1,0:T(8,128)(2,1)} async-done(((bf16[384,1792]{1,0:T(8,128)(2,1)}), bf16[96,1792]{1,0:T(8,128)(2,1)}) %reduce-scatter.15.cloned.1.call-update) | async-done | bytes 344080 | tf_op jit(solution)/shard_map/reduce_scatter | solution.py:57
  395.9 27.5 %reduce-scatter.11.cloned.1.call-done = bf16[96,1792]{1,0:T(8,128)(2,1)} async-done(((bf16[384,1792]{1,0:T(8,128)(2,1)}), bf16[96,1792]{1,0:T(8,128)(2,1)}) %reduce-scatter.11.cloned.1.call-update) | async-done | bytes 344080 | tf_op jit(solution)/shard_map/reduce_scatter | solution.py:45
  423.5 2.5 fusion.11
  426.0 0.0 all-gather.21.cloned.1.call-update
  426.0 0.0 all-gather.23.cloned.1.call-start
  426.1 0.5 all-gather.23.cloned.1.call-update
  426.6 0.0 all-gather.15.cloned.1.call-start
  426.6 0.7 all-gather.15.cloned.1.call-update
  427.3 0.0 reduce-scatter.19.cloned.1.call-start
  427.4 23.6 %all-gather.21.cloned.1.call-done = bf16[384,1792]{1,0:T(8,128)(2,1)} async-done(((bf16[96,1792]{1,0:T(8,128)(2,1)}), bf16[384,1792]{1,0:T(8,128)(2,1)}) %all-gather.21.cloned.1.call-update) | async-done | bytes 1376272 | tf_op jit(solution)/shard_map/all_gather | solution.py:62
  451.0 7.4 fusion
  458.4 0.0 reduce-scatter.19.cloned.1.call-update
  458.4 0.0 reduce-scatter.21.cloned.1.call-start
  458.5 20.5 %all-gather.23.cloned.1.call-done = bf16[384,1792]{1,0:T(8,128)(2,1)} async-done(((bf16[96,1792]{1,0:T(8,128)(2,1)}), bf16[384,1792]{1,0:T(8,128)(2,1)}) %all-gather.23.cloned.1.call-update) | async-done | bytes 1376272 | tf_op jit(solution)/shard_map/all_gather | solution.py:63
  479.0 7.5 fusion.1
  486.4 0.0 reduce-scatter.21.cloned.1.call-update
  486.5 0.2 reduce-scatter.13.cloned.1.call-start
  486.7 20.4 %all-gather.15.cloned.1.call-done = bf16[384,1792]{1,0:T(8,128)(2,1)} async-done(((bf16[96,1792]{1,0:T(8,128)(2,1)}), bf16[384,1792]{1,0:T(8,128)(2,1)}) %all-gather.15.cloned.1.call-update) | async-done | bytes 1376272 | tf_op jit(solution)/shard_map/all_gather | solution.py:50
  507.1 7.7 convolution_convert_fusion.4
  514.8 0.0 reduce-scatter.13.cloned.1.call-update
  514.8 0.0 reduce-scatter.17.cloned.1.call-start
  514.9 1.3 copy-done.2
  516.1 5.5 fusion.12
  521.6 0.0 copy-done.4
  521.7 9.2 %add_convert_fusion = bf16[384,2048]{1,0:T(8,128)(2,1)} fusion(f32[384,2048]{1,0:T(8,128)S(1)} %fusion.12, bf16[384,1792]{1,0:T(8,128)(2,1)S(1)} %copy-done.4, bf16[2048,1792]{1,0:T(8,128)(2,1)} %all-gather.13.cloned.1.call-done), kind=kOutput, calls=%fused_computation.5 | convolution fusion | flops 2820145152 | bytes 13434880 | tf_op jit(solution)/shard_map/dot_general | solution.py:12
  530.8 0.0 reduce-scatter.17.cloned.1.call-update
  530.9 0.0 reduce-scatter.23.cloned.1.call-start
  530.9 1.4 copy-done
  532.3 6.1 convolution_convert_fusion
  538.4 0.0 reduce-scatter.23.cloned.1.call-update
  538.4 42.8 %reduce-scatter.19.cloned.1.call-done = bf16[512,1792]{0,1:T(8,128)(2,1)} async-done(((bf16[2048,1792]{0,1:T(8,128)(2,1)}), bf16[512,1792]{0,1:T(8,128)(2,1)}) %reduce-scatter.19.cloned.1.call-update) | async-done | bytes 1835024 | tf_op jit(solution)/shard_map/reduce_scatter | solution.py:72
  581.2 3.8 copy.10
  585.0 70.9 %reduce-scatter.21.cloned.1.call-done = bf16[512,1792]{0,1:T(8,128)(2,1)} async-done(((bf16[2048,1792]{0,1:T(8,128)(2,1)}), bf16[512,1792]{0,1:T(8,128)(2,1)}) %reduce-scatter.21.cloned.1.call-update) | async-done | bytes 1835024 | tf_op jit(solution)/shard_map/reduce_scatter | solution.py:75
  655.8 3.8 copy.11
  659.6 76.2 %reduce-scatter.13.cloned.1.call-done = bf16[48,2048]{1,0:T(8,128)(2,1)} async-done(((bf16[384,2048]{1,0:T(8,128)(2,1)}), bf16[48,2048]{1,0:T(8,128)(2,1)}) %reduce-scatter.13.cloned.1.call-update) | async-done | bytes 196624 | tf_op jit(solution)/shard_map/reduce_scatter | solution.py:52
  735.9 77.8 %reduce-scatter.17.cloned.1.call-done = bf16[48,2048]{1,0:T(8,128)(2,1)} async-done(((bf16[384,2048]{1,0:T(8,128)(2,1)}), bf16[48,2048]{1,0:T(8,128)(2,1)}) %reduce-scatter.17.cloned.1.call-update) | async-done | bytes 196624 | tf_op jit(solution)/shard_map/reduce_scatter | solution.py:66
  813.6 72.8 %reduce-scatter.23.cloned.1.call-done = bf16[1792,512]{1,0:T(8,128)(2,1)} async-done(((bf16[1792,2048]{1,0:T(8,128)(2,1)}), bf16[1792,512]{1,0:T(8,128)(2,1)}) %reduce-scatter.23.cloned.1.call-update) | async-done | bytes 1835024 | tf_op jit(solution)/shard_map/reduce_scatter | solution.py:80
  (6 shorter events, 0.0 us)
Async XLA Ops:
  7.2 56.9 %all-gather.9.cloned.1.call-start = ((), (), s32[]{:S(2)}) async-start(), calls=%async_computation.8 | async-start | bytes 1769472 | tf_op jit(solution)/shard_map/all_gather | solution.py:33
  7.9 128.2 %all-gather.11.cloned.1.call-start = ((), (), s32[]{:S(2)}) async-start(), calls=%async_computation.9 | async-start | bytes 9175040 | tf_op jit(solution)/shard_map/all_gather | solution.py:35
  8.6 182.9 %all-gather.19.cloned.1.call-start = ((), (), s32[]{:S(2)}) async-start(), calls=%async_computation.16 | async-start | bytes 1769472 | tf_op jit(solution)/shard_map/all_gather | solution.py:55
  9.4 254.1 %all-gather.17.cloned.1.call-start = ((), (), s32[]{:S(2)}) async-start(), calls=%async_computation.14 | async-start | bytes 9175040 | tf_op jit(solution)/shard_map/all_gather | solution.py:38
  10.0 328.7 %all-gather.13.cloned.1.call-start = ((), (), s32[]{:S(2)}) async-start(), calls=%async_computation.11 | async-start | bytes 9175040 | tf_op jit(solution)/shard_map/all_gather | solution.py:36
  10.5 357.7 %reduce-scatter.9.cloned.1.call-start = ((), (), s32[]{:S(2)}) async-start(), calls=%async_computation.10 | async-start | bytes 1720320 | tf_op jit(solution)/shard_map/reduce_scatter | solution.py:42
  143.7 194.9 %copy-start.1 = (bf16[384,2048]{1,0:T(8,128)(2,1)S(1)}, bf16[384,2048]{1,0:T(8,128)(2,1)}, u32[]{:S(2)}) copy-start(bf16[384,2048]{1,0:T(8,128)(2,1)} %all-gather.9.cloned.1.call-done) | copy-start | bytes 4718596
  143.7 252.2 %reduce-scatter.15.cloned.1.call-start = ((), (), s32[]{:S(2)}) async-start(), calls=%async_computation.17 | async-start | bytes 1720320 | tf_op jit(solution)/shard_map/reduce_scatter | solution.py:57
  271.2 152.3 %reduce-scatter.11.cloned.1.call-start = ((), (), s32[]{:S(2)}) async-start(), calls=%async_computation.12 | async-start | bytes 1720320 | tf_op jit(solution)/shard_map/reduce_scatter | solution.py:45
  345.8 105.2 %all-gather.21.cloned.1.call-start = ((), (), s32[]{:S(2)}) async-start(), calls=%async_computation.18 | async-start | bytes 1720320 | tf_op jit(solution)/shard_map/all_gather | solution.py:62
  426.0 53.0 %all-gather.23.cloned.1.call-start = ((), (), s32[]{:S(2)}) async-start(), calls=%async_computation.19 | async-start | bytes 1720320 | tf_op jit(solution)/shard_map/all_gather | solution.py:63
  426.6 80.5 %all-gather.15.cloned.1.call-start = ((), (), s32[]{:S(2)}) async-start(), calls=%async_computation.13 | async-start | bytes 1720320 | tf_op jit(solution)/shard_map/all_gather | solution.py:50
  427.3 153.8 %reduce-scatter.19.cloned.1.call-start = ((), (), s32[]{:S(2)}) async-start(), calls=%async_computation.21 | async-start | bytes 9175040 | tf_op jit(solution)/shard_map/reduce_scatter | solution.py:72
  458.4 197.4 %reduce-scatter.21.cloned.1.call-start = ((), (), s32[]{:S(2)}) async-start(), calls=%async_computation.22 | async-start | bytes 9175040 | tf_op jit(solution)/shard_map/reduce_scatter | solution.py:75
  486.5 249.4 %reduce-scatter.13.cloned.1.call-start = ((), (), s32[]{:S(2)}) async-start(), calls=%async_computation.15 | async-start | bytes 1769472 | tf_op jit(solution)/shard_map/reduce_scatter | solution.py:52
  514.8 1.3 copy-start.2
  514.8 298.8 %reduce-scatter.17.cloned.1.call-start = ((), (), s32[]{:S(2)}) async-start(), calls=%async_computation.20 | async-start | bytes 1769472 | tf_op jit(solution)/shard_map/reduce_scatter | solution.py:66
  516.1 5.5 copy-start.4
  521.7 9.3 %copy-start.3 = (bf16[384,1792]{1,0:T(8,128)(2,1)S(1)}, bf16[384,1792]{1,0:T(8,128)(2,1)}, u32[]{:S(2)}) copy-start(bf16[384,1792]{1,0:T(8,128)(2,1)} %all-gather.15.cloned.1.call-done) | copy-start | bytes 4128772
  530.8 1.5 copy-start
  530.9 355.6 %reduce-scatter.23.cloned.1.call-start = ((), (), s32[]{:S(2)}) async-start(), calls=%async_computation.23 | async-start | bytes 9175040 | tf_op jit(solution)/shard_map/reduce_scatter | solution.py:80
Sparse Core Ops, SparseCore 0:
  10.3 53.7 all-gather.8
  65.7 70.2 all-gather.10
  138.4 53.1 all-gather.18
  193.1 70.2 all-gather.16
  265.0 73.6 all-gather.12
  341.5 26.7 reduce-scatter.8
  371.4 24.5 reduce-scatter.14
  398.9 24.4 reduce-scatter.10
  426.1 24.8 all-gather.20
  453.2 25.7 all-gather.22
  481.3 25.7 all-gather.14
  509.5 71.6 reduce-scatter.18
  583.7 72.0 reduce-scatter.20
  660.5 75.3 reduce-scatter.12
  740.5 73.0 reduce-scatter.16
  816.6 69.7 reduce-scatter.22
where the time goes:
time: 894 us; the launch traced here: 893 us
  waiting for transfers between devices  800 us (89%)
  matrix products  65.8 us (7%)
  between operations  14 us (2%)
  local copies, waits for them, and re-layouts  10.3 us (1%)
    reduce_scatter x1, waiting for transfers between devices, body(): lax.psum_scatter(input_part.astype(jnp.bfloat16), 'inw', scatter_dimensio...  77.8 us
    reduce_scatter x1, waiting for transfers between devices, body(): lax.psum_scatter(output_part.astype(jnp.bfloat16), 'inw', scatter_dimensi...  76.2 us
    reduce_scatter x1, waiting for transfers between devices, body(): lax.psum_scatter(down_weight_part.astype(jnp.bfloat16), 'depth', scatter_...  72.8 us
    all_gather x1, waiting for transfers between devices, body(): lax.all_gather(w_gate, 'depth', axis=0, tiled=True)  72 us
    all_gather x1, waiting for transfers between devices, body(): down_full = lax.all_gather(w_down, 'depth', axis=1, tiled=True)  71.8 us
    reduce_scatter x1, waiting for transfers between devices, body(): lax.psum_scatter(up_weight_part.astype(jnp.bfloat16), 'depth', scatter_di...  70.9 us
    all_gather x1, waiting for transfers between devices, body(): lax.all_gather(w_up, 'depth', axis=0, tiled=True)  67.4 us
    all_gather x1, waiting for transfers between devices, body(): input_rows = lax.all_gather(inputs, 'inw', axis=0, tiled=True)  53.5 us
  transfers between devices with their start and end apart: 16, of which 16 were waited for; matrix products, arithmetic and copies ran while one was open for 8% of the time, Pallas kernels for 0%

commit v1 on v0

v1 whole, which is shorter than its diff:
```python
import jax
import jax.numpy as jnp
from jax import lax
from jax.sharding import PartitionSpec as P

BF16, F32 = jnp.bfloat16, jnp.float32
STREAMS = 3
ORDERS = (("a", "b", "z"), ("b", "z", "a"), ("z", "a", "b"))


def dot(left, right, dims):
    return lax.dot_general(left, right, (dims, ((), ())), preferred_element_type=F32).astype(BF16)


def swap(value, axis, size, flip):
    return lax.ppermute(value, axis, [(i, i ^ flip) for i in range(size)])


def swap_core(value):
    return swap(value, "depth", 4, 1)


def swap_zlo(value):
    return swap(value, "depth", 4, 2)


def swap_zhi(value):
    return swap(value, "inw", 8, 4)


def swap_zboth(value):
    return lax.ppermute(value, ("depth", "inw"), [(i, i ^ 0b10100) for i in range(32)])


def swap_x(value, flip):
    return swap(value, "inw", 8, flip)


def swap_link(value, link):
    if link == "z":
        return swap_zlo(value)
    return swap(value, "outw", 4, 1 if link == "a" else 3)


def add(*terms):
    total = terms[0].astype(F32)
    for term in terms[1:]:
        total = total + term.astype(F32)
    return total


def either(bit, if_zero, if_one):
    return jnp.where(bit == 0, if_zero, if_one)


def ordered(bit, own, other, axis):
    return either(bit, jnp.concatenate([own, other], axis), jnp.concatenate([other, own], axis))


def half(value, index):
    size = value.shape[0] // 2
    return lax.dynamic_slice_in_dim(value, index * size, size, 0)


def reduce_rows(part, links, bits):
    value = part
    for link in links:
        received = swap_link(half(value, 1 - bits[link]), link)
        value = add(half(value, bits[link]), received)
        if link != links[-1]:
            value = value.astype(BF16)
    return value


def gather_rows(value, links, bits):
    for link in links[::-1]:
        value = ordered(bits[link], value, swap_link(value, link), 0)
    return value


def gather_tokens(local, zlo, core):
    rows = local.reshape(STREAMS, 16, 2048)

    def columns(z, c):
        return lax.dynamic_slice_in_dim(rows, (z * 2 + c) * 512, 512, 2)

    keep = jnp.concatenate([columns(zlo, core), columns(zlo, 1 - core)], 2)
    give = jnp.concatenate([columns(1 - zlo, core), columns(1 - zlo, 1 - core)], 2)
    from_lo, from_hi, from_both = swap_zlo(give), swap_zhi(keep), swap_zboth(give)
    own = jnp.concatenate([ordered(zlo, keep, from_lo, 1), ordered(zlo, from_hi, from_both, 1)], 1)
    first, third = swap_x(own, 1), swap_x(own, 3)
    top, bottom = swap_x(third[:, :32], 1), swap_x(first[:, 32:], 3)
    return jnp.concatenate([own, first, third, top, bottom], 1)


def scatter_tokens(part, zlo, core):
    own, first, third, top, bottom = (
        part[:, 0:64], part[:, 64:128], part[:, 128:192], part[:, 192:224], part[:, 224:256],
    )
    to_third, to_first = swap_x(top, 1), swap_x(bottom, 3)
    first = jnp.concatenate([first[:, :32], add(first[:, 32:], to_first).astype(BF16)], 1)
    third = jnp.concatenate([add(third[:, :32], to_third).astype(BF16), third[:, 32:]], 1)
    own = add(own, swap_x(first, 1), swap_x(third, 3)).astype(BF16)
    near, far = own[:, :32], own[:, 32:]

    def rows_of(value, z):
        return lax.dynamic_slice_in_dim(value, z * 16, 16, 1)

    from_lo = swap_zlo(rows_of(near, 1 - zlo))
    from_hi = swap_zhi(rows_of(far, zlo))
    from_both = swap_zboth(rows_of(far, 1 - zlo))
    mine = add(rows_of(near, zlo), from_hi).astype(BF16)
    other = add(from_lo, from_both).astype(BF16)

    def unswapped(value):
        return ordered(core, value[:, :, :512], value[:, :, 512:], 2)

    out = ordered(zlo, unswapped(mine), unswapped(other), 2)
    return out.reshape(STREAMS * 16, 2048)


def body(inputs, w_gate, w_up, w_down, cotangent):
    depth, outw = lax.axis_index("depth"), lax.axis_index("outw")
    zlo, core = depth >> 1, depth & 1
    bits = {"a": (outw & 1) ^ (outw >> 1), "b": outw >> 1, "z": zlo}

    x_all = gather_tokens(inputs, zlo, core)
    cot_all = gather_tokens(cotangent, zlo, core)
    gate_up = jnp.concatenate(
        [
            jnp.concatenate([w_gate, swap_core(w_gate)], 0),
            jnp.concatenate([w_up, swap_core(w_up)], 0),
        ],
        1,
    )
    down = jnp.concatenate([w_down, swap_core(w_down)], 1)

    sums = [
        reduce_rows(dot(x_all[s], gate_up, ((1,), (0,))), ORDERS[s], bits) for s in range(STREAMS)
    ]
    hidden_grads = [
        reduce_rows(dot(cot_all[s], down, ((1,), (1,))), ORDERS[s], bits) for s in range(STREAMS)
    ]
    hidden, acts = [], []
    for s in range(STREAMS):
        gate_sum, up_sum = sums[s][:, :1792], sums[s][:, 1792:]
        local = (jax.nn.silu(gate_sum) * up_sum).astype(BF16)
        hidden.append(gather_rows(local, ORDERS[s], bits))
    for s in range(STREAMS):
        gate_sum, up_sum = sums[s][:, :1792], sums[s][:, 1792:]
        grad_hidden = hidden_grads[s]
        sigmoid_gate = jax.nn.sigmoid(gate_sum)
        grad_gate_act = (
            grad_hidden * up_sum * sigmoid_gate * (1.0 + gate_sum * (1.0 - sigmoid_gate))
        ).astype(BF16)
        grad_up_act = (grad_hidden * gate_sum * sigmoid_gate).astype(BF16)
        local = jnp.concatenate([grad_gate_act, grad_up_act], 1)
        acts.append(gather_rows(local, ORDERS[s], bits))

    output_part = jnp.stack([dot(h, down, ((1,), (0,))) for h in hidden])
    outputs = scatter_tokens(output_part, zlo, core)
    input_part = jnp.stack([dot(a, gate_up, ((1,), (1,))) for a in acts])
    grad_inputs = scatter_tokens(input_part, zlo, core)

    hidden_all = jnp.concatenate(hidden, 0)
    acts_all = jnp.concatenate(acts, 0)
    x_rows = x_all.reshape(768, 1024)
    cot_rows = cot_all.reshape(768, 1024)
    down_other = swap_core(dot(hidden_all, cot_rows[:, 512:], ((0,), (0,))))
    grad_down = add(dot(hidden_all, cot_rows[:, :512], ((0,), (0,))), down_other).astype(BF16)
    act_other = swap_core(dot(x_rows[:, 512:], acts_all, ((0,), (0,))))
    act_own = dot(x_rows[:, :512], acts_all, ((0,), (0,)))
    grad_gate = add(act_own[:, :1792], act_other[:, :1792]).astype(BF16)
    grad_up = add(act_own[:, 1792:], act_other[:, 1792:]).astype(BF16)
    return outputs, grad_inputs, grad_gate, grad_up, grad_down


def solution(mesh):
    tokens = P(("depth", "inw"), "outw")
    w_in = P(("outw", "depth"), "inw")
    w_out = P("inw", ("outw", "depth"))
    return jax.shard_map(
        body,
        mesh=mesh,
        in_specs=(tokens, w_in, w_in, w_out, tokens),
        out_specs=(tokens, tokens, w_in, w_in, w_out),
        check_vma=False,
    )
```

time: 894 us -> 283 us (0.32)
  waiting for transfers between devices: 800 us -> 123 us
  starting transfers between devices: 0.82 us -> 83.7 us
  matrix products: 65.8 us -> 30.6 us
  other arithmetic: 2.53 us -> 34.5 us
  between operations: 14 us -> 2.1 us
    reduce_scatter x8 -> x0, waiting for transfers between devices: 418 us -> none  [the longest x1 77.8 us: body(): lax.psum_scatter(input_part.astype(jnp.bfloat16), 'inw', scatter_dimensio...]
    all_gather x8 -> x0, waiting for transfers between devices: 377 us -> none  [the longest x1 72 us: body(): lax.all_gather(w_gate, 'depth', axis=0, tiled=True)]
    ppermute x0 -> x69, waiting for transfers between devices: none -> 123 us  [the longest x65 118 us: swap(): return lax.ppermute(value, axis, [(i, i ^ flip) for i in range(size)])]
    ppermute x0 -> x69, starting transfers between devices: none -> 83.7 us  [the longest x65 75.4 us: swap(): return lax.ppermute(value, axis, [(i, i ^ flip) for i in range(size)])]
    dot_general x9 -> x16, matrix products: 65.8 us -> 30.6 us  [dot(): lax.dot_general(left, right, (dims, ((), ())), preferred_element_type=F32)]
    concatenate x0 -> x12, other arithmetic: none -> 19.6 us  [the longest x1 17.8 us: body(): jnp.concatenate([jnp.concatenate([w_gate, swap_core(w_gate)], 0), jnp.con...]
  transfers between devices with their start and end apart: 16 -> 69, of which waited for: 16 -> 39; matrix products, arithmetic and copies ran while one was open for 8% -> 23% of each run, Pallas kernels for 0% -> 0%
where the time goes in v1:
time: 283 us; the launch traced here: 278 us
  waiting for transfers between devices  123 us (43%)
  starting transfers between devices  83.7 us (30%)
  other arithmetic  34.5 us (12%)
  matrix products  30.6 us (11%)
  local copies, waits for them, and re-layouts  4.25 us (2%)
    ppermute x65, waiting for transfers between devices, swap(): return lax.ppermute(value, axis, [(i, i ^ flip) for i in range(size)])  118 us
    ppermute x65, starting transfers between devices, swap(): return lax.ppermute(value, axis, [(i, i ^ flip) for i in range(size)])  75.4 us
    dot_general x16, matrix products, dot(): lax.dot_general(left, right, (dims, ((), ())), preferred_element_type=F32)  30.6 us
    concatenate x1, other arithmetic, body(): jnp.concatenate([jnp.concatenate([w_gate, swap_core(w_gate)], 0), jnp.con...  17.8 us
    ppermute x4, starting transfers between devices, swap_zboth(): lax.ppermute(value, ('depth', 'inw'), [(i, i ^ 20) for i in range(32)])  8.25 us
  transfers between devices with their start and end apart: 69, of which 39 were waited for; matrix products, arithmetic and copies ran while one was open for 23% of the time, Pallas kernels for 0%

profile of v1, /device:TPU:0, one launch (start us, length us, event | category | flops | bytes accessed | tf_op | source)
XLA Modules:
  0.0 278.2 jit_solution(5890109320524327044)
XLA Ops:
  1.8 4.2 %collective-permute-start.2 = (bf16[3,16,1024]{2,1,0:T(8,128)(2,1)S(1)}, bf16[3,16,1024]{2,1,0:T(8,128)(2,1)S(1)}, u32[]{:S(2)}, u32[]{:S(2)}) collective-permute-start(bf16[3,16,1024]{2,1,0:T(8,128)(2,1)S(1)} %pad_maximum_fusion.18), channel_id=1, source_target_pairs={{0,80},{4,84},{8,88},{12,92},{16,64},{20,68},{24,72},{28,76},{32,1... | collective-permute-start | bytes 294920 | tf_op jit(solution)/shard_map/ppermute | solution.py:32
  6.6 1.6 collective-permute-start.35
  8.2 2.7 collective-permute-start.36
  10.9 2.5 collective-permute-done.35
  16.4 2.8 collective-permute-start.39
  19.1 2.2 collective-permute-start.1
  22.1 3.6 %collective-permute-done.1 = bf16[3,16,1024]{2,1,0:T(8,128)(2,1)S(1)} collective-permute-done((bf16[3,16,1024]{2,1,0:T(8,128)(2,1)S(1)}, bf16[3,16,1024]{2,1,0:T(8,128)(2,1)S(1)}, u32[]{:S(2)}, u32[]{:S(2)}) %collective-permute-start.1) | collective-permute-done | bytes 98336 | tf_op jit(solution)/shard_map/ppermute | solution.py:16
  29.6 1.9 constant_dynamic-update-slice_fusion.7
  31.5 6.4 %collective-permute-done.38 = bf16[3,64,1024]{2,1,0:T(8,128)(2,1)S(1)} collective-permute-done((bf16[3,64,1024]{2,1,0:T(8,128)(2,1)}, bf16[3,64,1024]{2,1,0:T(8,128)(2,1)S(1)}, u32[]{:S(2)}, u32[]{:S(2)}) %collective-permute-start.38) | collective-permute-done | bytes 393248 | tf_op jit(solution)/shard_map/ppermute | solution.py:16
  39.6 6.8 %collective-permute-done.3 = bf16[3,64,1024]{2,1,0:T(8,128)(2,1)S(1)} collective-permute-done((bf16[3,64,1024]{2,1,0:T(8,128)(2,1)}, bf16[3,64,1024]{2,1,0:T(8,128)(2,1)S(1)}, u32[]{:S(2)}, u32[]{:S(2)}) %collective-permute-start.3) | collective-permute-done | bytes 393248 | tf_op jit(solution)/shard_map/ppermute | solution.py:16
  47.0 1.9 collective-permute-done.40
  49.2 4.0 %collective-permute-done.41 = bf16[3,32,1024]{2,1,0:T(8,128)(2,1)S(1)} collective-permute-done((bf16[3,32,1024]{2,1,0:T(8,128)(2,1)S(1)}, bf16[3,32,1024]{2,1,0:T(8,128)(2,1)S(1)}, u32[]{:S(2)}, u32[]{:S(2)}) %collective-permute-start.41) | collective-permute-done | bytes 196640 | tf_op jit(solution)/shard_map/ppermute | solution.py:16
  54.6 5.9 %collective-permute-done.6 = bf16[3,32,1024]{2,1,0:T(8,128)(2,1)S(1)} collective-permute-done((bf16[3,32,1024]{2,1,0:T(8,128)(2,1)S(1)}, bf16[3,32,1024]{2,1,0:T(8,128)(2,1)S(1)}, u32[]{:S(2)}, u32[]{:S(2)}) %collective-permute-start.6) | collective-permute-done | bytes 196640 | tf_op jit(solution)/shard_map/ppermute | solution.py:16
  60.6 17.8 %maximum_maximum_fusion = bf16[1024,3584]{1,0:T(8,128)(2,1)S(1)} fusion(bf16[512,1792]{1,0:T(8,128)(2,1)} %collective-permute-done.8, bf16[512,1792]{1,0:T(8,128)(2,1)S(1)} %copy-done, bf16[512,1792]{1,0:T(8,128)(2,1)} %collective-permute-done.7, bf16[512,1792]{1,0:T(8,128)(2,1)S(1)} %copy-done.1), kind=kLoop, calls=%fused_computation | loop fusion | flops 29360128 | bytes 14680064 | tf_op jit(solution)/shard_map/concatenate | solution.py:129
  78.4 2.1 convolution_convert_fusion.2
  80.5 2.1 convolution_convert_fusion.3
  82.6 2.1 convolution_convert_fusion.4
  88.1 3.1 %collective-permute-start.16 = (bf16[128,3584]{1,0:T(8,128)(2,1)S(1)}, bf16[128,3584]{1,0:T(8,128)(2,1)S(1)}, u32[]{:S(2)}, u32[]{:S(2)}) collective-permute-start(bf16[128,3584]{1,0:T(8,128)(2,1)S(1)} %constant_dynamic-slice_fusion.24), channel_id=1, source_target_pairs={{0,3},{1,2},{2,1},{3,0},{4,7},{5,6},{6,5},{7,4},{8,11},{9,10},{10,... | collective-permute-start | bytes 2752520 | tf_op jit(solution)/shard_map/ppermute | solution.py:16
  91.5 1.7 collective-permute-start.54
  95.6 18.5 %collective-permute-done.54 = bf16[128,1792]{1,0:T(8,128)(2,1)S(1)} collective-permute-done((bf16[128,1792]{1,0:T(8,128)(2,1)S(1)}, bf16[128,1792]{1,0:T(8,128)(2,1)S(1)}, u32[]{:S(2)}, u32[]{:S(2)}) %collective-permute-start.54) | collective-permute-done | bytes 458784 | tf_op jit(solution)/shard_map/ppermute | solution.py:16
  116.6 6.2 %collective-permute-done.42 = bf16[128,1792]{1,0:T(8,128)(2,1)S(1)} collective-permute-done((bf16[128,1792]{1,0:T(8,128)(2,1)S(1)}, bf16[128,1792]{1,0:T(8,128)(2,1)S(1)}, u32[]{:S(2)}, u32[]{:S(2)}) %collective-permute-start.42) | collective-permute-done | bytes 458784 | tf_op jit(solution)/shard_map/ppermute | solution.py:16
  123.5 1.7 collective-permute-done.55
  125.2 3.0 %collective-permute-start.43 = (bf16[64,1792]{1,0:T(8,128)(2,1)S(1)}, bf16[64,1792]{1,0:T(8,128)(2,1)S(1)}, u32[]{:S(2)}, u32[]{:S(2)}) collective-permute-start(bf16[64,1792]{1,0:T(8,128)(2,1)S(1)} %constant_dynamic-slice_fusion.10), channel_id=1, source_target_pairs={{0,3},{1,2},{2,1},{3,0},{4,7},{5,6},{6,5},{7,4},{8,11},{9,10},{10,... | collective-permute-start | bytes 688136 | tf_op jit(solution)/shard_map/ppermute | solution.py:16
  128.3 2.1 collective-permute-done.49
  130.4 3.2 %collective-permute-start.56 = (bf16[32,1792]{1,0:T(8,128)(2,1)S(1)}, bf16[32,1792]{1,0:T(8,128)(2,1)S(1)}, u32[]{:S(2)}, u32[]{:S(2)}) collective-permute-start(bf16[32,1792]{1,0:T(8,128)(2,1)S(1)} %constant_dynamic-slice_fusion.3), channel_id=1, source_target_pairs={{0,3},{1,2},{2,1},{3,0},{4,7},{5,6},{6,5},{7,4},{8,11},{9,10},{10,... | collective-permute-start | bytes 344072 | tf_op jit(solution)/shard_map/ppermute | solution.py:16
  134.3 2.1 collective-permute-start.23
  136.6 2.1 collective-permute-start.17
  139.0 4.5 %collective-permute-done.23 = bf16[64,3584]{1,0:T(8,128)(2,1)S(1)} collective-permute-done((bf16[64,3584]{1,0:T(8,128)(2,1)S(1)}, bf16[64,3584]{1,0:T(8,128)(2,1)S(1)}, u32[]{:S(2)}, u32[]{:S(2)}) %collective-permute-start.23) | collective-permute-done | bytes 458784 | tf_op jit(solution)/shard_map/ppermute | solution.py:16
  143.5 1.6 collective-permute-start.10
  145.3 2.1 collective-permute-start.24
  147.6 9.3 %collective-permute-done.10 = bf16[64,3584]{1,0:T(8,128)(2,1)S(1)} collective-permute-done((bf16[64,3584]{1,0:T(8,128)(2,1)S(1)}, bf16[64,3584]{1,0:T(8,128)(2,1)S(1)}, u32[]{:S(2)}, u32[]{:S(2)}) %collective-permute-start.10) | collective-permute-done | bytes 458784 | tf_op jit(solution)/shard_map/ppermute | solution.py:16
  157.2 2.2 collective-permute-done.24
  160.9 1.7 collective-permute-start.25
  162.6 1.6 collective-permute-done.18
  164.3 1.9 collective-permute-start.57
  168.9 1.8 collective-permute-start.12
  172.5 2.6 collective-permute-done.12
  179.8 1.8 collective-permute-start.46
  181.6 1.8 collective-permute-done.20
  187.4 7.3 %collective-permute-done.46 = bf16[64,3584]{1,0:T(8,128)(2,1)S(1)} collective-permute-done((bf16[64,3584]{1,0:T(8,128)(2,1)S(1)}, bf16[64,3584]{1,0:T(8,128)(2,1)S(1)}, u32[]{:S(2)}, u32[]{:S(2)}) %collective-permute-start.46) | collective-permute-done | bytes 458784 | tf_op jit(solution)/shard_map/ppermute | solution.py:16
  195.4 1.6 collective-permute-start.47
  206.8 2.9 %convolution_convert_fusion.5 = bf16[1792,512]{1,0:T(8,128)(2,1)} fusion(bf16[256,1792]{1,0:T(8,128)(2,1)S(1)} %maximum_select_fusion.5, bf16[256,1792]{1,0:T(8,128)(2,1)S(1)} %maximum_select_fusion.4, bf16[256,1792]{1,0:T(8,128)(2,1)S(1)} %maximum_select_fusion.3, bf16[768,1024]{1,0:T(8,128)(2,1)S(1)} %bitcast.62), kind=kOutput, calls=%fused_computation.10 | convolution fusion | flops 1418461184 | bytes 5373952 | tf_op jit(solution)/shard_map/dot_general | solution.py:12
  209.8 2.1 collective-permute-done.28
  212.8 2.2 collective-permute-start.31
  215.0 1.6 convolution_convert_fusion.6
  216.6 3.4 %collective-permute-done.29 = bf16[3,64,1024]{2,1,0:T(8,128)(2,1)S(1)} collective-permute-done((bf16[3,64,1024]{2,1,0:T(8,128)(2,1)S(1)}, bf16[3,64,1024]{2,1,0:T(8,128)(2,1)S(1)}, u32[]{:S(2)}, u32[]{:S(2)}) %collective-permute-start.29) | collective-permute-done | bytes 393248 | tf_op jit(solution)/shard_map/ppermute | solution.py:16
  220.0 1.7 collective-permute-done.31
  222.0 2.8 %collective-permute-start.32 = (bf16[3,16,1024]{2,1,0:T(8,128)(2,1)S(1)}, bf16[3,16,1024]{2,1,0:T(8,128)(2,1)S(1)}, u32[]{:S(2)}, u32[]{:S(2)}) collective-permute-start(bf16[3,16,1024]{2,1,0:T(8,128)(2,1)S(1)} %get-tuple-element.46), channel_id=1, source_target_pairs={{0,16},{4,20},{8,24},{12,28},{16,0},{20,4},{24,8},{28,12},{1,17},{... | collective-permute-start | bytes 294920 | tf_op jit(solution)/shard_map/ppermute | solution.py:16
  225.6 2.6 collective-permute-done.32
  228.2 2.6 collective-permute-start.34
  231.2 2.9 %collective-permute-done.34 = bf16[3,16,1024]{2,1,0:T(8,128)(2,1)S(1)} collective-permute-done((bf16[3,16,1024]{2,1,0:T(8,128)(2,1)S(1)}, bf16[3,16,1024]{2,1,0:T(8,128)(2,1)S(1)}, u32[]{:S(2)}, u32[]{:S(2)}) %collective-permute-start.34) | collective-permute-done | bytes 98336 | tf_op jit(solution)/shard_map/ppermute | solution.py:32
  235.3 2.1 fusion
  237.8 2.1 fusion.1
  240.3 2.1 fusion.2
  242.4 2.3 collective-permute-start.60
  244.8 3.3 %convolution_convert_fusion = bf16[512,3584]{1,0:T(8,128)(2,1)S(1)} fusion(bf16[256,3584]{1,0:T(8,128)(2,1)S(1)} %maximum_select_fusion.2, bf16[256,3584]{1,0:T(8,128)(2,1)S(1)} %maximum_select_fusion.1, bf16[256,3584]{1,0:T(8,128)(2,1)S(1)} %maximum_select_fusion, bf16[768,1024]{1,0:T(8,128)(2,1)S(1)} %bitcast.64), kind=kOutput, calls=%fused_computation.1 | convolution fusion | flops 2836922368 | bytes 9961472 | tf_op jit(solution)/shard_map/dot_general | solution.py:12
  252.0 3.3 %convolution_convert_fusion.1 = bf16[512,3584]{1,0:T(8,128)(2,1)S(1)} fusion(bf16[256,3584]{1,0:T(8,128)(2,1)S(1)} %maximum_select_fusion.2, bf16[256,3584]{1,0:T(8,128)(2,1)S(1)} %maximum_select_fusion.1, bf16[256,3584]{1,0:T(8,128)(2,1)S(1)} %maximum_select_fusion, bf16[768,1024]{1,0:T(8,128)(2,1)S(1)} %bitcast.65), kind=kOutput, calls=%fused_computation.2 | convolution fusion | flops 2836922368 | bytes 9961472 | tf_op jit(solution)/shard_map/dot_general | solution.py:12
  255.5 4.8 %collective-permute-done.61 = bf16[3,64,1024]{2,1,0:T(8,128)(2,1)S(1)} collective-permute-done((bf16[3,64,1024]{2,1,0:T(8,128)(2,1)S(1)}, bf16[3,64,1024]{2,1,0:T(8,128)(2,1)S(1)}, u32[]{:S(2)}, u32[]{:S(2)}) %collective-permute-start.61) | collective-permute-done | bytes 393248 | tf_op jit(solution)/shard_map/ppermute | solution.py:16
  260.3 2.7 collective-permute-done.63
  264.7 1.9 collective-permute-start.65
  267.5 2.2 collective-permute-done.64
  270.3 2.1 collective-permute-done.66
  273.3 1.7 add_convert_fusion
  275.0 2.7 add_convert_fusion.1
  (215 shorter events, 61.8 us)
Async XLA Ops:
  1.8 24.1 %collective-permute-start.2 = (bf16[3,16,1024]{2,1,0:T(8,128)(2,1)S(1)}, bf16[3,16,1024]{2,1,0:T(8,128)(2,1)S(1)}, u32[]{:S(2)}, u32[]{:S(2)}) collective-permute-start(bf16[3,16,1024]{2,1,0:T(8,128)(2,1)S(1)} %pad_maximum_fusion.18), channel_id=1, source_target_pairs={{0,80},{4,84},{8,88},{12,92},{16,64},{20,68},{24,72},{28,76},{32,1... | collective-permute-start | bytes 294920 | tf_op jit(solution)/shard_map/ppermute | solution.py:32
  6.0 13.1 %collective-permute-start = (bf16[3,16,1024]{2,1,0:T(8,128)(2,1)S(1)}, bf16[3,16,1024]{2,1,0:T(8,128)(2,1)S(1)}, u32[]{:S(2)}, u32[]{:S(2)}) collective-permute-start(bf16[3,16,1024]{2,1,0:T(8,128)(2,1)S(1)} %pad_maximum_fusion.18), channel_id=1, source_target_pairs={{0,64},{32,96},{64,0},{96,32},{1,65},{33,97},{65,1},{97,33},{2,66}... | collective-permute-start | bytes 294920 | tf_op jit(solution)/shard_map/ppermute | solution.py:16
  6.0 8.8 %collective-permute-start.37 = (bf16[3,16,1024]{2,1,0:T(8,128)(2,1)S(1)}, bf16[3,16,1024]{2,1,0:T(8,128)(2,1)S(1)}, u32[]{:S(2)}, u32[]{:S(2)}) collective-permute-start(bf16[3,16,1024]{2,1,0:T(8,128)(2,1)S(1)} %pad_maximum_fusion.20), channel_id=1, source_target_pairs={{0,80},{4,84},{8,88},{12,92},{16,64},{20,68},{24,72},{28,76},{32,1... | collective-permute-start | bytes 294920 | tf_op jit(solution)/shard_map/ppermute | solution.py:32
  6.6 6.8 %collective-permute-start.35 = (bf16[3,16,1024]{2,1,0:T(8,128)(2,1)S(1)}, bf16[3,16,1024]{2,1,0:T(8,128)(2,1)S(1)}, u32[]{:S(2)}, u32[]{:S(2)}) collective-permute-start(bf16[3,16,1024]{2,1,0:T(8,128)(2,1)S(1)} %pad_maximum_fusion.20), channel_id=1, source_target_pairs={{0,64},{32,96},{64,0},{96,32},{1,65},{33,97},{65,1},{97,33},{2,66}... | collective-permute-start | bytes 294920 | tf_op jit(solution)/shard_map/ppermute | solution.py:16
  8.2 6.6 %collective-permute-start.36 = (bf16[3,16,1024]{2,1,0:T(8,128)(2,1)S(1)}, bf16[3,16,1024]{2,1,0:T(8,128)(2,1)S(1)}, u32[]{:S(2)}, u32[]{:S(2)}) collective-permute-start(bf16[3,16,1024]{2,1,0:T(8,128)(2,1)S(1)} %pad_maximum_fusion.19), channel_id=1, source_target_pairs={{0,16},{4,20},{8,24},{12,28},{16,0},{20,4},{24,8},{28,12},{1,17},{... | collective-permute-start | bytes 294920 | tf_op jit(solution)/shard_map/ppermute | solution.py:16
  13.4 47.1 %collective-permute-start.7 = (bf16[512,1792]{1,0:T(8,128)(2,1)}, bf16[512,1792]{1,0:T(8,128)(2,1)}, u32[]{:S(2)}, u32[]{:S(2)}) collective-permute-start(bf16[512,1792]{1,0:T(8,128)(2,1)} %param.6), channel_id=1, source_target_pairs={{0,32},{32,0},{64,96},{96,64},{1,33},{33,1},{65,97},{97,65},{2,34}... | collective-permute-start | bytes 5505032 | tf_op jit(solution)/shard_map/ppermute | solution.py:16
  14.9 45.7 %collective-permute-start.8 = (bf16[512,1792]{1,0:T(8,128)(2,1)S(1)}, bf16[512,1792]{1,0:T(8,128)(2,1)}, u32[]{:S(2)}, u32[]{:S(2)}) collective-permute-start(bf16[512,1792]{1,0:T(8,128)(2,1)S(1)} %copy-done), channel_id=1, source_target_pairs={{0,32},{32,0},{64,96},{96,64},{1,33},{33,1},{65,97},{97,65},{2,34}... | collective-permute-start | bytes 5505032 | tf_op jit(solution)/shard_map/ppermute | solution.py:16
  16.4 12.9 %collective-permute-start.39 = (bf16[3,64,1024]{2,1,0:T(8,128)(2,1)}, bf16[3,64,1024]{2,1,0:T(8,128)(2,1)S(1)}, u32[]{:S(2)}, u32[]{:S(2)}) collective-permute-start(bf16[3,64,1024]{2,1,0:T(8,128)(2,1)} %pad_maximum_fusion.9), channel_id=1, source_target_pairs={{0,12},{4,8},{8,4},{12,0},{16,28},{20,24},{24,20},{28,16},{1,13},{... | collective-permute-start | bytes 1179656 | tf_op jit(solution)/shard_map/ppermute | solution.py:16
  19.1 6.5 %collective-permute-start.1 = (bf16[3,16,1024]{2,1,0:T(8,128)(2,1)S(1)}, bf16[3,16,1024]{2,1,0:T(8,128)(2,1)S(1)}, u32[]{:S(2)}, u32[]{:S(2)}) collective-permute-start(bf16[3,16,1024]{2,1,0:T(8,128)(2,1)S(1)} %pad_maximum_fusion.17), channel_id=1, source_target_pairs={{0,16},{4,20},{8,24},{12,28},{16,0},{20,4},{24,8},{28,12},{1,17},{... | collective-permute-start | bytes 294920 | tf_op jit(solution)/shard_map/ppermute | solution.py:16
  25.6 12.3 %collective-permute-start.38 = (bf16[3,64,1024]{2,1,0:T(8,128)(2,1)}, bf16[3,64,1024]{2,1,0:T(8,128)(2,1)S(1)}, u32[]{:S(2)}, u32[]{:S(2)}) collective-permute-start(bf16[3,64,1024]{2,1,0:T(8,128)(2,1)} %pad_maximum_fusion.9), channel_id=1, source_target_pairs={{0,4},{4,0},{8,12},{12,8},{16,20},{20,16},{24,28},{28,24},{1,5},{5... | collective-permute-start | bytes 1179656 | tf_op jit(solution)/shard_map/ppermute | solution.py:16
  27.4 11.6 %collective-permute-start.4 = (bf16[3,64,1024]{2,1,0:T(8,128)(2,1)}, bf16[3,64,1024]{2,1,0:T(8,128)(2,1)S(1)}, u32[]{:S(2)}, u32[]{:S(2)}) collective-permute-start(bf16[3,64,1024]{2,1,0:T(8,128)(2,1)} %pad_maximum_fusion.8), channel_id=1, source_target_pairs={{0,12},{4,8},{8,4},{12,0},{16,28},{20,24},{24,20},{28,16},{1,13},{... | collective-permute-start | bytes 1179656 | tf_op jit(solution)/shard_map/ppermute | solution.py:16
  29.3 17.0 %collective-permute-start.3 = (bf16[3,64,1024]{2,1,0:T(8,128)(2,1)}, bf16[3,64,1024]{2,1,0:T(8,128)(2,1)S(1)}, u32[]{:S(2)}, u32[]{:S(2)}) collective-permute-start(bf16[3,64,1024]{2,1,0:T(8,128)(2,1)} %pad_maximum_fusion.8), channel_id=1, source_target_pairs={{0,4},{4,0},{8,12},{12,8},{16,20},{20,16},{24,28},{28,24},{1,5},{5... | collective-permute-start | bytes 1179656 | tf_op jit(solution)/shard_map/ppermute | solution.py:16
  37.9 46.8 %collective-permute-start.15 = (bf16[1792,512]{1,0:T(8,128)(2,1)S(1)}, bf16[1792,512]{1,0:T(8,128)(2,1)S(1)}, u32[]{:S(2)}, u32[]{:S(2)}) collective-permute-start(bf16[1792,512]{1,0:T(8,128)(2,1)S(1)} %copy-done.2), channel_id=1, source_target_pairs={{0,32},{32,0},{64,96},{96,64},{1,33},{33,1},{65,97},{97,65},{2,34}... | collective-permute-start | bytes 5505032 | tf_op jit(solution)/shard_map/ppermute | solution.py:16
  39.0 9.9 %collective-permute-start.40 = (bf16[3,32,1024]{2,1,0:T(8,128)(2,1)S(1)}, bf16[3,32,1024]{2,1,0:T(8,128)(2,1)S(1)}, u32[]{:S(2)}, u32[]{:S(2)}) collective-permute-start(bf16[3,32,1024]{2,1,0:T(8,128)(2,1)S(1)} %slice.240), channel_id=1, source_target_pairs={{0,4},{4,0},{8,12},{12,8},{16,20},{20,16},{24,28},{28,24},{1,5},{5... | collective-permute-start | bytes 589832 | tf_op jit(solution)/shard_map/ppermute | solution.py:16
  46.3 6.9 %collective-permute-start.41 = (bf16[3,32,1024]{2,1,0:T(8,128)(2,1)S(1)}, bf16[3,32,1024]{2,1,0:T(8,128)(2,1)S(1)}, u32[]{:S(2)}, u32[]{:S(2)}) collective-permute-start(bf16[3,32,1024]{2,1,0:T(8,128)(2,1)S(1)} %slice.241), channel_id=1, source_target_pairs={{0,12},{4,8},{8,4},{12,0},{16,28},{20,24},{24,20},{28,16},{1,13},{... | collective-permute-start | bytes 589832 | tf_op jit(solution)/shard_map/ppermute | solution.py:16
  53.2 7.3 %collective-permute-start.6 = (bf16[3,32,1024]{2,1,0:T(8,128)(2,1)S(1)}, bf16[3,32,1024]{2,1,0:T(8,128)(2,1)S(1)}, u32[]{:S(2)}, u32[]{:S(2)}) collective-permute-start(bf16[3,32,1024]{2,1,0:T(8,128)(2,1)S(1)} %slice.223), channel_id=1, source_target_pairs={{0,12},{4,8},{8,4},{12,0},{16,28},{20,24},{24,20},{28,16},{1,13},{... | collective-permute-start | bytes 589832 | tf_op jit(solution)/shard_map/ppermute | solution.py:16
  87.4 46.5 %collective-permute-start.22 = (bf16[128,3584]{1,0:T(8,128)(2,1)S(1)}, bf16[128,3584]{1,0:T(8,128)(2,1)S(1)}, u32[]{:S(2)}, u32[]{:S(2)}) collective-permute-start(bf16[128,3584]{1,0:T(8,128)(2,1)S(1)} %constant_dynamic-slice_fusion.21), channel_id=1, source_target_pairs={{0,64},{32,96},{64,0},{96,32},{1,65},{33,97},{65,1},{97,33},{2,66}... | collective-permute-start | bytes 2752520 | tf_op jit(solution)/shard_map/ppermute | solution.py:16
  88.1 46.2 %collective-permute-start.16 = (bf16[128,3584]{1,0:T(8,128)(2,1)S(1)}, bf16[128,3584]{1,0:T(8,128)(2,1)S(1)}, u32[]{:S(2)}, u32[]{:S(2)}) collective-permute-start(bf16[128,3584]{1,0:T(8,128)(2,1)S(1)} %constant_dynamic-slice_fusion.24), channel_id=1, source_target_pairs={{0,3},{1,2},{2,1},{3,0},{4,7},{5,6},{6,5},{7,4},{8,11},{9,10},{10,... | collective-permute-start | bytes 2752520 | tf_op jit(solution)/shard_map/ppermute | solution.py:16
  91.3 45.4 %collective-permute-start.9 = (bf16[128,3584]{1,0:T(8,128)(2,1)S(1)}, bf16[128,3584]{1,0:T(8,128)(2,1)S(1)}, u32[]{:S(2)}, u32[]{:S(2)}) collective-permute-start(bf16[128,3584]{1,0:T(8,128)(2,1)S(1)} %constant_dynamic-slice_fusion.27), channel_id=1, source_target_pairs={{0,1},{1,0},{2,3},{3,2},{4,5},{5,4},{6,7},{7,6},{8,9},{9,8},{10,11... | collective-permute-start | bytes 2752520 | tf_op jit(solution)/shard_map/ppermute | solution.py:16
  91.5 22.7 %collective-permute-start.54 = (bf16[128,1792]{1,0:T(8,128)(2,1)S(1)}, bf16[128,1792]{1,0:T(8,128)(2,1)S(1)}, u32[]{:S(2)}, u32[]{:S(2)}) collective-permute-start(bf16[128,1792]{1,0:T(8,128)(2,1)S(1)} %constant_dynamic-slice_fusion.5), channel_id=1, source_target_pairs={{0,64},{32,96},{64,0},{96,32},{1,65},{33,97},{65,1},{97,33},{2,66}... | collective-permute-start | bytes 1376264 | tf_op jit(solution)/shard_map/ppermute | solution.py:16
  93.3 22.6 %collective-permute-start.48 = (bf16[128,1792]{1,0:T(8,128)(2,1)S(1)}, bf16[128,1792]{1,0:T(8,128)(2,1)S(1)}, u32[]{:S(2)}, u32[]{:S(2)}) collective-permute-start(bf16[128,1792]{1,0:T(8,128)(2,1)S(1)} %constant_dynamic-slice_fusion.8), channel_id=1, source_target_pairs={{0,3},{1,2},{2,1},{3,0},{4,7},{5,6},{6,5},{7,4},{8,11},{9,10},{10,... | collective-permute-start | bytes 1376264 | tf_op jit(solution)/shard_map/ppermute | solution.py:16
  114.2 8.6 %collective-permute-start.42 = (bf16[128,1792]{1,0:T(8,128)(2,1)S(1)}, bf16[128,1792]{1,0:T(8,128)(2,1)S(1)}, u32[]{:S(2)}, u32[]{:S(2)}) collective-permute-start(bf16[128,1792]{1,0:T(8,128)(2,1)S(1)} %constant_dynamic-slice_fusion.11), channel_id=1, source_target_pairs={{0,1},{1,0},{2,3},{3,2},{4,5},{5,4},{6,7},{7,6},{8,9},{9,8},{10,11... | collective-permute-start | bytes 1376264 | tf_op jit(solution)/shard_map/ppermute | solution.py:16
  115.9 9.3 %collective-permute-start.55 = (bf16[64,1792]{1,0:T(8,128)(2,1)S(1)}, bf16[64,1792]{1,0:T(8,128)(2,1)S(1)}, u32[]{:S(2)}, u32[]{:S(2)}) collective-permute-start(bf16[64,1792]{1,0:T(8,128)(2,1)S(1)} %constant_dynamic-slice_fusion.4), channel_id=1, source_target_pairs={{0,1},{1,0},{2,3},{3,2},{4,5},{5,4},{6,7},{7,6},{8,9},{9,8},{10,11... | collective-permute-start | bytes 688136 | tf_op jit(solution)/shard_map/ppermute | solution.py:16
  122.7 7.6 %collective-permute-start.49 = (bf16[64,1792]{1,0:T(8,128)(2,1)S(1)}, bf16[64,1792]{1,0:T(8,128)(2,1)S(1)}, u32[]{:S(2)}, u32[]{:S(2)}) collective-permute-start(bf16[64,1792]{1,0:T(8,128)(2,1)S(1)} %constant_dynamic-slice_fusion.7), channel_id=1, source_target_pairs={{0,64},{32,96},{64,0},{96,32},{1,65},{33,97},{65,1},{97,33},{2,66}... | collective-permute-start | bytes 688136 | tf_op jit(solution)/shard_map/ppermute | solution.py:16
  125.2 8.5 %collective-permute-start.43 = (bf16[64,1792]{1,0:T(8,128)(2,1)S(1)}, bf16[64,1792]{1,0:T(8,128)(2,1)S(1)}, u32[]{:S(2)}, u32[]{:S(2)}) collective-permute-start(bf16[64,1792]{1,0:T(8,128)(2,1)S(1)} %constant_dynamic-slice_fusion.10), channel_id=1, source_target_pairs={{0,3},{1,2},{2,1},{3,0},{4,7},{5,6},{6,5},{7,4},{8,11},{9,10},{10,... | collective-permute-start | bytes 688136 | tf_op jit(solution)/shard_map/ppermute | solution.py:16
  130.4 30.4 %collective-permute-start.56 = (bf16[32,1792]{1,0:T(8,128)(2,1)S(1)}, bf16[32,1792]{1,0:T(8,128)(2,1)S(1)}, u32[]{:S(2)}, u32[]{:S(2)}) collective-permute-start(bf16[32,1792]{1,0:T(8,128)(2,1)S(1)} %constant_dynamic-slice_fusion.3), channel_id=1, source_target_pairs={{0,3},{1,2},{2,1},{3,0},{4,7},{5,6},{6,5},{7,4},{8,11},{9,10},{10,... | collective-permute-start | bytes 344072 | tf_op jit(solution)/shard_map/ppermute | solution.py:16
  133.7 32.6 %collective-permute-start.50 = (bf16[32,1792]{1,0:T(8,128)(2,1)S(1)}, bf16[32,1792]{1,0:T(8,128)(2,1)S(1)}, u32[]{:S(2)}, u32[]{:S(2)}) collective-permute-start(bf16[32,1792]{1,0:T(8,128)(2,1)S(1)} %constant_dynamic-slice_fusion.6), channel_id=1, source_target_pairs={{0,1},{1,0},{2,3},{3,2},{4,5},{5,4},{6,7},{7,6},{8,9},{9,8},{10,11... | collective-permute-start | bytes 344072 | tf_op jit(solution)/shard_map/ppermute | solution.py:16
  133.9 34.8 %collective-permute-start.44 = (bf16[32,1792]{1,0:T(8,128)(2,1)S(1)}, bf16[32,1792]{1,0:T(8,128)(2,1)S(1)}, u32[]{:S(2)}, u32[]{:S(2)}) collective-permute-start(bf16[32,1792]{1,0:T(8,128)(2,1)S(1)} %constant_dynamic-slice_fusion.9), channel_id=1, source_target_pairs={{0,64},{32,96},{64,0},{96,32},{1,65},{33,97},{65,1},{97,33},{2,66}... | collective-permute-start | bytes 344072 | tf_op jit(solution)/shard_map/ppermute | solution.py:16
  134.3 9.2 %collective-permute-start.23 = (bf16[64,3584]{1,0:T(8,128)(2,1)S(1)}, bf16[64,3584]{1,0:T(8,128)(2,1)S(1)}, u32[]{:S(2)}, u32[]{:S(2)}) collective-permute-start(bf16[64,3584]{1,0:T(8,128)(2,1)S(1)} %constant_dynamic-slice_fusion.20), channel_id=1, source_target_pairs={{0,1},{1,0},{2,3},{3,2},{4,5},{5,4},{6,7},{7,6},{8,9},{9,8},{10,11... | collective-permute-start | bytes 1376264 | tf_op jit(solution)/shard_map/ppermute | solution.py:16
  136.6 8.6 %collective-permute-start.17 = (bf16[64,3584]{1,0:T(8,128)(2,1)S(1)}, bf16[64,3584]{1,0:T(8,128)(2,1)S(1)}, u32[]{:S(2)}, u32[]{:S(2)}) collective-permute-start(bf16[64,3584]{1,0:T(8,128)(2,1)S(1)} %constant_dynamic-slice_fusion.23), channel_id=1, source_target_pairs={{0,64},{32,96},{64,0},{96,32},{1,65},{33,97},{65,1},{97,33},{2,66}... | collective-permute-start | bytes 1376264 | tf_op jit(solution)/shard_map/ppermute | solution.py:16
  143.5 13.4 %collective-permute-start.10 = (bf16[64,3584]{1,0:T(8,128)(2,1)S(1)}, bf16[64,3584]{1,0:T(8,128)(2,1)S(1)}, u32[]{:S(2)}, u32[]{:S(2)}) collective-permute-start(bf16[64,3584]{1,0:T(8,128)(2,1)S(1)} %constant_dynamic-slice_fusion.26), channel_id=1, source_target_pairs={{0,3},{1,2},{2,1},{3,0},{4,7},{5,6},{6,5},{7,4},{8,11},{9,10},{10,... | collective-permute-start | bytes 1376264 | tf_op jit(solution)/shard_map/ppermute | solution.py:16
  145.3 14.0 %collective-permute-start.24 = (bf16[32,3584]{1,0:T(8,128)(2,1)S(1)}, bf16[32,3584]{1,0:T(8,128)(2,1)S(1)}, u32[]{:S(2)}, u32[]{:S(2)}) collective-permute-start(bf16[32,3584]{1,0:T(8,128)(2,1)S(1)} %constant_dynamic-slice_fusion.19), channel_id=1, source_target_pairs={{0,3},{1,2},{2,1},{3,0},{4,7},{5,6},{6,5},{7,4},{8,11},{9,10},{10,... | collective-permute-start | bytes 688136 | tf_op jit(solution)/shard_map/ppermute | solution.py:16
  156.9 7.4 %collective-permute-start.18 = (bf16[32,3584]{1,0:T(8,128)(2,1)S(1)}, bf16[32,3584]{1,0:T(8,128)(2,1)S(1)}, u32[]{:S(2)}, u32[]{:S(2)}) collective-permute-start(bf16[32,3584]{1,0:T(8,128)(2,1)S(1)} %constant_dynamic-slice_fusion.22), channel_id=1, source_target_pairs={{0,1},{1,0},{2,3},{3,2},{4,5},{5,4},{6,7},{7,6},{8,9},{9,8},{10,11... | collective-permute-start | bytes 688136 | tf_op jit(solution)/shard_map/ppermute | solution.py:16
  159.3 8.5 %collective-permute-start.11 = (bf16[32,3584]{1,0:T(8,128)(2,1)S(1)}, bf16[32,3584]{1,0:T(8,128)(2,1)S(1)}, u32[]{:S(2)}, u32[]{:S(2)}) collective-permute-start(bf16[32,3584]{1,0:T(8,128)(2,1)S(1)} %constant_dynamic-slice_fusion.25), channel_id=1, source_target_pairs={{0,64},{32,96},{64,0},{96,32},{1,65},{33,97},{65,1},{97,33},{2,66}... | collective-permute-start | bytes 688136 | tf_op jit(solution)/shard_map/ppermute | solution.py:16
  160.9 9.8 %collective-permute-start.25 = (bf16[32,1792]{1,0:T(8,128)(2,1)S(1)}, bf16[32,1792]{1,0:T(8,128)(2,1)S(1)}, u32[]{:S(2)}, u32[]{:S(2)}) collective-permute-start(bf16[32,1792]{1,0:T(8,128)(2,1)S(1)} %get-tuple-element.35), channel_id=1, source_target_pairs={{0,3},{1,2},{2,1},{3,0},{4,7},{5,6},{6,5},{7,4},{8,11},{9,10},{10,... | collective-permute-start | bytes 344072 | tf_op jit(solution)/shard_map/ppermute | solution.py:16
  164.3 12.2 %collective-permute-start.57 = (bf16[32,3584]{1,0:T(8,128)(2,1)S(1)}, bf16[32,3584]{1,0:T(8,128)(2,1)S(1)}, u32[]{:S(2)}, u32[]{:S(2)}) collective-permute-start(bf16[32,3584]{1,0:T(8,128)(2,1)S(1)} %pad_maximum_fusion.12), channel_id=1, source_target_pairs={{0,3},{1,2},{2,1},{3,0},{4,7},{5,6},{6,5},{7,4},{8,11},{9,10},{10,... | collective-permute-start | bytes 688136 | tf_op jit(solution)/shard_map/ppermute | solution.py:16
  167.8 9.6 %collective-permute-start.51 = (bf16[32,3584]{1,0:T(8,128)(2,1)S(1)}, bf16[32,3584]{1,0:T(8,128)(2,1)S(1)}, u32[]{:S(2)}, u32[]{:S(2)}) collective-permute-start(bf16[32,3584]{1,0:T(8,128)(2,1)S(1)} %pad_maximum_fusion.11), channel_id=1, source_target_pairs={{0,1},{1,0},{2,3},{3,2},{4,5},{5,4},{6,7},{7,6},{8,9},{9,8},{10,11... | collective-permute-start | bytes 688136 | tf_op jit(solution)/shard_map/ppermute | solution.py:16
  168.9 6.2 %collective-permute-start.12 = (bf16[32,1792]{1,0:T(8,128)(2,1)S(1)}, bf16[32,1792]{1,0:T(8,128)(2,1)S(1)}, u32[]{:S(2)}, u32[]{:S(2)}) collective-permute-start(bf16[32,1792]{1,0:T(8,128)(2,1)S(1)} %get-tuple-element.33), channel_id=1, source_target_pairs={{0,64},{32,96},{64,0},{96,32},{1,65},{33,97},{65,1},{97,33},{2,66}... | collective-permute-start | bytes 344072 | tf_op jit(solution)/shard_map/ppermute | solution.py:16
  170.7 7.8 %collective-permute-start.45 = (bf16[32,3584]{1,0:T(8,128)(2,1)S(1)}, bf16[32,3584]{1,0:T(8,128)(2,1)S(1)}, u32[]{:S(2)}, u32[]{:S(2)}) collective-permute-start(bf16[32,3584]{1,0:T(8,128)(2,1)S(1)} %pad_maximum_fusion.10), channel_id=1, source_target_pairs={{0,64},{32,96},{64,0},{96,32},{1,65},{33,97},{65,1},{97,33},{2,66}... | collective-permute-start | bytes 688136 | tf_op jit(solution)/shard_map/ppermute | solution.py:16
  171.3 8.5 %collective-permute-start.26 = (bf16[64,1792]{1,0:T(8,128)(2,1)S(1)}, bf16[64,1792]{1,0:T(8,128)(2,1)S(1)}, u32[]{:S(2)}, u32[]{:S(2)}) collective-permute-start(bf16[64,1792]{1,0:T(8,128)(2,1)S(1)} %maximum_select_fusion.17), channel_id=1, source_target_pairs={{0,1},{1,0},{2,3},{3,2},{4,5},{5,4},{6,7},{7,6},{8,9},{9,8},{10,11... | collective-permute-start | bytes 688136 | tf_op jit(solution)/shard_map/ppermute | solution.py:16
  175.0 8.4 %collective-permute-start.20 = (bf16[64,1792]{1,0:T(8,128)(2,1)S(1)}, bf16[64,1792]{1,0:T(8,128)(2,1)S(1)}, u32[]{:S(2)}, u32[]{:S(2)}) collective-permute-start(bf16[64,1792]{1,0:T(8,128)(2,1)S(1)} %maximum_select_fusion.16), channel_id=1, source_target_pairs={{0,64},{32,96},{64,0},{96,32},{1,65},{33,97},{65,1},{97,33},{2,66}... | collective-permute-start | bytes 688136 | tf_op jit(solution)/shard_map/ppermute | solution.py:16
  176.4 9.8 %collective-permute-start.13 = (bf16[64,1792]{1,0:T(8,128)(2,1)S(1)}, bf16[64,1792]{1,0:T(8,128)(2,1)S(1)}, u32[]{:S(2)}, u32[]{:S(2)}) collective-permute-start(bf16[64,1792]{1,0:T(8,128)(2,1)S(1)} %maximum_select_fusion.15), channel_id=1, source_target_pairs={{0,3},{1,2},{2,1},{3,0},{4,7},{5,6},{6,5},{7,4},{8,11},{9,10},{10,... | collective-permute-start | bytes 688136 | tf_op jit(solution)/shard_map/ppermute | solution.py:16
  177.4 19.7 %collective-permute-start.58 = (bf16[64,3584]{1,0:T(8,128)(2,1)S(1)}, bf16[64,3584]{1,0:T(8,128)(2,1)S(1)}, u32[]{:S(2)}, u32[]{:S(2)}) collective-permute-start(bf16[64,3584]{1,0:T(8,128)(2,1)S(1)} %maximum_select_fusion.14), channel_id=1, source_target_pairs={{0,1},{1,0},{2,3},{3,2},{4,5},{5,4},{6,7},{7,6},{8,9},{9,8},{10,11... | collective-permute-start | bytes 1376264 | tf_op jit(solution)/shard_map/ppermute | solution.py:16
  178.5 16.8 %collective-permute-start.52 = (bf16[64,3584]{1,0:T(8,128)(2,1)S(1)}, bf16[64,3584]{1,0:T(8,128)(2,1)S(1)}, u32[]{:S(2)}, u32[]{:S(2)}) collective-permute-start(bf16[64,3584]{1,0:T(8,128)(2,1)S(1)} %maximum_select_fusion.13), channel_id=1, source_target_pairs={{0,64},{32,96},{64,0},{96,32},{1,65},{33,97},{65,1},{97,33},{2,66}... | collective-permute-start | bytes 1376264 | tf_op jit(solution)/shard_map/ppermute | solution.py:16
  179.8 14.9 %collective-permute-start.46 = (bf16[64,3584]{1,0:T(8,128)(2,1)S(1)}, bf16[64,3584]{1,0:T(8,128)(2,1)S(1)}, u32[]{:S(2)}, u32[]{:S(2)}) collective-permute-start(bf16[64,3584]{1,0:T(8,128)(2,1)S(1)} %maximum_select_fusion.12), channel_id=1, source_target_pairs={{0,3},{1,2},{2,1},{3,0},{4,7},{5,6},{6,5},{7,4},{8,11},{9,10},{10,... | collective-permute-start | bytes 1376264 | tf_op jit(solution)/shard_map/ppermute | solution.py:16
  183.4 16.8 %collective-permute-start.27 = (bf16[128,1792]{1,0:T(8,128)(2,1)S(1)}, bf16[128,1792]{1,0:T(8,128)(2,1)S(1)}, u32[]{:S(2)}, u32[]{:S(2)}) collective-permute-start(bf16[128,1792]{1,0:T(8,128)(2,1)S(1)} %maximum_select_fusion.11), channel_id=1, source_target_pairs={{0,64},{32,96},{64,0},{96,32},{1,65},{33,97},{65,1},{97,33},{2,66}... | collective-permute-start | bytes 1376264 | tf_op jit(solution)/shard_map/ppermute | solution.py:16
  186.3 16.0 %collective-permute-start.21 = (bf16[128,1792]{1,0:T(8,128)(2,1)S(1)}, bf16[128,1792]{1,0:T(8,128)(2,1)S(1)}, u32[]{:S(2)}, u32[]{:S(2)}) collective-permute-start(bf16[128,1792]{1,0:T(8,128)(2,1)S(1)} %maximum_select_fusion.10), channel_id=1, source_target_pairs={{0,3},{1,2},{2,1},{3,0},{4,7},{5,6},{6,5},{7,4},{8,11},{9,10},{10,... | collective-permute-start | bytes 1376264 | tf_op jit(solution)/shard_map/ppermute | solution.py:16
  194.7 8.9 %collective-permute-start.14 = (bf16[128,1792]{1,0:T(8,128)(2,1)S(1)}, bf16[128,1792]{1,0:T(8,128)(2,1)S(1)}, u32[]{:S(2)}, u32[]{:S(2)}) collective-permute-start(bf16[128,1792]{1,0:T(8,128)(2,1)S(1)} %maximum_select_fusion.9), channel_id=1, source_target_pairs={{0,1},{1,0},{2,3},{3,2},{4,5},{5,4},{6,7},{7,6},{8,9},{9,8},{10,11... | collective-permute-start | bytes 1376264 | tf_op jit(solution)/shard_map/ppermute | solution.py:16
  195.4 39.5 %collective-permute-start.47 = (bf16[128,3584]{1,0:T(8,128)(2,1)S(1)}, bf16[128,3584]{1,0:T(8,128)(2,1)S(1)}, u32[]{:S(2)}, u32[]{:S(2)}) collective-permute-start(bf16[128,3584]{1,0:T(8,128)(2,1)S(1)} %maximum_select_fusion.6), channel_id=1, source_target_pairs={{0,1},{1,0},{2,3},{3,2},{4,5},{5,4},{6,7},{7,6},{8,9},{9,8},{10,11... | collective-permute-start | bytes 2752520 | tf_op jit(solution)/shard_map/ppermute | solution.py:16
  197.1 40.3 %collective-permute-start.53 = (bf16[128,3584]{1,0:T(8,128)(2,1)S(1)}, bf16[128,3584]{1,0:T(8,128)(2,1)S(1)}, u32[]{:S(2)}, u32[]{:S(2)}) collective-permute-start(bf16[128,3584]{1,0:T(8,128)(2,1)S(1)} %maximum_select_fusion.7), channel_id=1, source_target_pairs={{0,3},{1,2},{2,1},{3,0},{4,7},{5,6},{6,5},{7,4},{8,11},{9,10},{10,... | collective-permute-start | bytes 2752520 | tf_op jit(solution)/shard_map/ppermute | solution.py:16
  200.2 39.7 %collective-permute-start.59 = (bf16[128,3584]{1,0:T(8,128)(2,1)S(1)}, bf16[128,3584]{1,0:T(8,128)(2,1)S(1)}, u32[]{:S(2)}, u32[]{:S(2)}) collective-permute-start(bf16[128,3584]{1,0:T(8,128)(2,1)S(1)} %maximum_select_fusion.8), channel_id=1, source_target_pairs={{0,64},{32,96},{64,0},{96,32},{1,65},{33,97},{65,1},{97,33},{2,66}... | collective-permute-start | bytes 2752520 | tf_op jit(solution)/shard_map/ppermute | solution.py:16
  205.0 7.0 %collective-permute-start.28 = (bf16[3,32,1024]{2,1,0:T(8,128)(2,1)S(1)}, bf16[3,32,1024]{2,1,0:T(8,128)(2,1)S(1)}, u32[]{:S(2)}, u32[]{:S(2)}) collective-permute-start(bf16[3,32,1024]{2,1,0:T(8,128)(2,1)S(1)} %get-tuple-element.25), channel_id=1, source_target_pairs={{0,12},{4,8},{8,4},{12,0},{16,28},{20,24},{24,20},{28,16},{1,13},{... | collective-permute-start | bytes 589832 | tf_op jit(solution)/shard_map/ppermute | solution.py:16
  205.6 6.4 %collective-permute-start.30 = (bf16[3,32,1024]{2,1,0:T(8,128)(2,1)S(1)}, bf16[3,32,1024]{2,1,0:T(8,128)(2,1)S(1)}, u32[]{:S(2)}, u32[]{:S(2)}) collective-permute-start(bf16[3,32,1024]{2,1,0:T(8,128)(2,1)S(1)} %get-tuple-element.26), channel_id=1, source_target_pairs={{0,4},{4,0},{8,12},{12,8},{16,20},{20,16},{24,28},{28,24},{1,5},{5... | collective-permute-start | bytes 589832 | tf_op jit(solution)/shard_map/ppermute | solution.py:16
  212.2 7.9 %collective-permute-start.29 = (bf16[3,64,1024]{2,1,0:T(8,128)(2,1)S(1)}, bf16[3,64,1024]{2,1,0:T(8,128)(2,1)S(1)}, u32[]{:S(2)}, u32[]{:S(2)}) collective-permute-start(bf16[3,64,1024]{2,1,0:T(8,128)(2,1)S(1)} %get-tuple-element.21), channel_id=1, source_target_pairs={{0,4},{4,0},{8,12},{12,8},{16,20},{20,16},{24,28},{28,24},{1,5},{5... | collective-permute-start | bytes 1179656 | tf_op jit(solution)/shard_map/ppermute | solution.py:16
  212.8 9.0 %collective-permute-start.31 = (bf16[3,64,1024]{2,1,0:T(8,128)(2,1)S(1)}, bf16[3,64,1024]{2,1,0:T(8,128)(2,1)S(1)}, u32[]{:S(2)}, u32[]{:S(2)}) collective-permute-start(bf16[3,64,1024]{2,1,0:T(8,128)(2,1)S(1)} %get-tuple-element.22), channel_id=1, source_target_pairs={{0,12},{4,8},{8,4},{12,0},{16,28},{20,24},{24,20},{28,16},{1,13},{... | collective-permute-start | bytes 1179656 | tf_op jit(solution)/shard_map/ppermute | solution.py:16
  222.0 6.2 %collective-permute-start.32 = (bf16[3,16,1024]{2,1,0:T(8,128)(2,1)S(1)}, bf16[3,16,1024]{2,1,0:T(8,128)(2,1)S(1)}, u32[]{:S(2)}, u32[]{:S(2)}) collective-permute-start(bf16[3,16,1024]{2,1,0:T(8,128)(2,1)S(1)} %get-tuple-element.46), channel_id=1, source_target_pairs={{0,16},{4,20},{8,24},{12,28},{16,0},{20,4},{24,8},{28,12},{1,17},{... | collective-permute-start | bytes 294920 | tf_op jit(solution)/shard_map/ppermute | solution.py:16
  224.8 6.0 %collective-permute-start.33 = (bf16[3,16,1024]{2,1,0:T(8,128)(2,1)S(1)}, bf16[3,16,1024]{2,1,0:T(8,128)(2,1)S(1)}, u32[]{:S(2)}, u32[]{:S(2)}) collective-permute-start(bf16[3,16,1024]{2,1,0:T(8,128)(2,1)S(1)} %constant_dynamic-slice_fusion.17), channel_id=1, source_target_pairs={{0,64},{32,96},{64,0},{96,32},{1,65},{33,97},{65,1},{97,33},{2,66}... | collective-permute-start | bytes 294920 | tf_op jit(solution)/shard_map/ppermute | solution.py:16
  228.2 5.8 %collective-permute-start.34 = (bf16[3,16,1024]{2,1,0:T(8,128)(2,1)S(1)}, bf16[3,16,1024]{2,1,0:T(8,128)(2,1)S(1)}, u32[]{:S(2)}, u32[]{:S(2)}) collective-permute-start(bf16[3,16,1024]{2,1,0:T(8,128)(2,1)S(1)} %get-tuple-element.47), channel_id=1, source_target_pairs={{0,80},{4,84},{8,88},{12,92},{16,64},{20,68},{24,72},{28,76},{32,1... | collective-permute-start | bytes 294920 | tf_op jit(solution)/shard_map/ppermute | solution.py:32
  230.8 42.4 %collective-permute-start.68 = (bf16[1792,512]{1,0:T(8,128)(2,1)}, bf16[1792,512]{1,0:T(8,128)(2,1)S(1)}, u32[]{:S(2)}, u32[]{:S(2)}) collective-permute-start(bf16[1792,512]{1,0:T(8,128)(2,1)} %convolution_convert_fusion.5), channel_id=1, source_target_pairs={{0,32},{32,0},{64,96},{96,64},{1,33},{33,1},{65,97},{97,65},{2,34}... | collective-permute-start | bytes 5505032 | tf_op jit(solution)/shard_map/ppermute | solution.py:16
  242.4 7.0 %collective-permute-start.60 = (bf16[3,32,1024]{2,1,0:T(8,128)(2,1)S(1)}, bf16[3,32,1024]{2,1,0:T(8,128)(2,1)S(1)}, u32[]{:S(2)}, u32[]{:S(2)}) collective-permute-start(bf16[3,32,1024]{2,1,0:T(8,128)(2,1)S(1)} %get-tuple-element.19), channel_id=1, source_target_pairs={{0,12},{4,8},{8,4},{12,0},{16,28},{20,24},{24,20},{28,16},{1,13},{... | collective-permute-start | bytes 589832 | tf_op jit(solution)/shard_map/ppermute | solution.py:16
  248.1 26.9 %collective-permute-start.67 = (bf16[512,3584]{1,0:T(8,128)(2,1)S(1)}, bf16[512,3584]{1,0:T(8,128)(2,1)S(1)}, u32[]{:S(2)}, u32[]{:S(2)}) collective-permute-start(bf16[512,3584]{1,0:T(8,128)(2,1)S(1)} %convolution_convert_fusion), channel_id=1, source_target_pairs={{0,32},{32,0},{64,96},{96,64},{1,33},{33,1},{65,97},{97,65},{2,34}... | collective-permute-start | bytes 11010056 | tf_op jit(solution)/shard_map/ppermute | solution.py:16
  250.7 9.6 %collective-permute-start.61 = (bf16[3,64,1024]{2,1,0:T(8,128)(2,1)S(1)}, bf16[3,64,1024]{2,1,0:T(8,128)(2,1)S(1)}, u32[]{:S(2)}, u32[]{:S(2)}) collective-permute-start(bf16[3,64,1024]{2,1,0:T(8,128)(2,1)S(1)} %get-tuple-element.15), channel_id=1, source_target_pairs={{0,4},{4,0},{8,12},{12,8},{16,20},{20,16},{24,28},{28,24},{1,5},{5... | collective-permute-start | bytes 1179656 | tf_op jit(solution)/shard_map/ppermute | solution.py:16
  250.7 12.2 %collective-permute-start.63 = (bf16[3,64,1024]{2,1,0:T(8,128)(2,1)S(1)}, bf16[3,64,1024]{2,1,0:T(8,128)(2,1)S(1)}, u32[]{:S(2)}, u32[]{:S(2)}) collective-permute-start(bf16[3,64,1024]{2,1,0:T(8,128)(2,1)S(1)} %get-tuple-element.16), channel_id=1, source_target_pairs={{0,12},{4,8},{8,4},{12,0},{16,28},{20,24},{24,20},{28,16},{1,13},{... | collective-permute-start | bytes 1179656 | tf_op jit(solution)/shard_map/ppermute | solution.py:16
  263.2 6.5 %collective-permute-start.64 = (bf16[3,16,1024]{2,1,0:T(8,128)(2,1)S(1)}, bf16[3,16,1024]{2,1,0:T(8,128)(2,1)S(1)}, u32[]{:S(2)}, u32[]{:S(2)}) collective-permute-start(bf16[3,16,1024]{2,1,0:T(8,128)(2,1)S(1)} %get-tuple-element.40), channel_id=1, source_target_pairs={{0,16},{4,20},{8,24},{12,28},{16,0},{20,4},{24,8},{28,12},{1,17},{... | collective-permute-start | bytes 294920 | tf_op jit(solution)/shard_map/ppermute | solution.py:16
  (10 other events, 96.5 us)
